TPU v7x, 512 devices: a whole 4x8x8 slice. The times are simulated.
512 devices in a mesh: seq: 512 (over x, y, z, core).
Axes of the slice: x: 4, y: 8, z: 8, core: 2. Of those that a mesh axis runs over, the one named last changes fastest.
Arguments:
- queries: bfloat16 [262144, 1024], P('seq'), may hold values from -60 to 60
- keys: bfloat16 [262144, 1024], P('seq'), may hold values from -60 to 60
- values: bfloat16 [262144, 1024], P('seq'), may hold values from -6 to 6
- lengths: int32 [512], P('seq'), may hold values from 64 to 512
Outputs:
- attended: bfloat16 [262144, 1024], P('seq')
All inputs are finite; a program needn't handle non-finite values.
Results may differ from a plain program's by a relative error of at most 0.0056.
Values may be sent and summed in bfloat16 or wider, within the bound.
A program may use at most 64 MiB of HBM per device.

v0:
```python
import math

import jax
import jax.numpy as jnp
from jax import lax
from jax.sharding import PartitionSpec as P

HEADS = 16
HEAD_DIM = 64


def passed_along(block, axis, distance):
    devices = range(lax.axis_size(axis))
    route = [((i - distance) % len(devices), i) for i in devices]
    return lax.ppermute(block, axis, route)


def attend_block(query_block, key_block, value_block, length):
    row_count = query_block.shape[0]
    key_count = key_block.shape[0]
    group_heads = 4
    slab_width = group_heads * HEAD_DIM
    passes = HEADS // group_heads
    score_scale = 1.0 / math.sqrt(HEAD_DIM)
    visible = jnp.arange(key_count) < length

    def head_pass(group_index, state_pair):
        outputs, log_sums = state_pair
        first_column = group_index * slab_width
        query_slab = lax.dynamic_slice_in_dim(query_block, first_column, slab_width, 1).reshape(
            row_count, group_heads, HEAD_DIM
        )
        key_slab = lax.dynamic_slice_in_dim(key_block, first_column, slab_width, 1).reshape(
            key_count, group_heads, HEAD_DIM
        )
        value_slab = lax.dynamic_slice_in_dim(value_block, first_column, slab_width, 1).reshape(
            key_count, group_heads, HEAD_DIM
        )
        scores = (
            jnp.einsum("thd,shd->hts", query_slab, key_slab, preferred_element_type=jnp.float32)
            * score_scale
        )
        scores = jnp.where(visible[None, None, :], scores, -1e30)
        row_peaks = jnp.max(scores, axis=-1)
        weights = jnp.exp(scores - row_peaks[..., None]).astype(jnp.bfloat16)
        totals = jnp.sum(weights.astype(jnp.float32), axis=-1)
        blended = jnp.einsum(
            "hts,shd->thd", weights, value_slab, preferred_element_type=jnp.float32
        )
        blended = blended / jnp.transpose(totals)[:, :, None]
        outputs = lax.dynamic_update_slice_in_dim(
            outputs, blended.reshape(row_count, slab_width).astype(jnp.bfloat16), first_column, 1
        )
        log_sums = lax.dynamic_update_slice_in_dim(
            log_sums, row_peaks + jnp.log(totals), group_index * group_heads, 0
        )
        return (outputs, log_sums)

    initial = (
        jnp.zeros((row_count, HEADS * HEAD_DIM), jnp.bfloat16),
        jnp.zeros((HEADS, row_count), jnp.float32),
    )
    return lax.fori_loop(0, passes, head_pass, initial)


def combine(partials):
    log_sums = jnp.stack([partial_value[1] for partial_value in partials])
    ceiling = jnp.max(log_sums, axis=0)
    shares = jnp.exp(log_sums - ceiling[None])
    share_total = jnp.sum(shares, axis=0)
    row_count = partials[0][0].shape[0]
    mixture = jnp.zeros((row_count, HEADS, HEAD_DIM), jnp.float32)
    for position, partial_value in enumerate(partials):
        piece_heads = partial_value[0].astype(jnp.float32).reshape(row_count, HEADS, HEAD_DIM)
        mixture = mixture + piece_heads * jnp.transpose(shares[position])[:, :, None]
    mixture = mixture / jnp.transpose(share_total)[:, :, None]
    return mixture.reshape(row_count, HEADS * HEAD_DIM).astype(jnp.bfloat16)


def reply_round(queries, keys, values, lengths, distance):
    far_queries, far_keys, far_values, far_lengths = passed_along(
        (queries, keys, values, lengths), "seq", distance
    )
    local_part = attend_block(queries, far_keys, far_values, far_lengths[0])
    theirs = attend_block(far_queries, keys, values, lengths[0])
    back_out = passed_along(theirs[0], "seq", -distance)
    back_lse = passed_along(theirs[1], "seq", -distance)
    return [local_part, (back_out, back_lse)]


def local(queries, keys, values, lengths):
    partials = [attend_block(queries, keys, values, lengths[0])]
    distance_far = lax.axis_size("seq") // 4
    for distance in (1, distance_far):
        partials = partials + reply_round(queries, keys, values, lengths, distance)
    return combine(partials)


def solution(mesh):
    return jax.shard_map(
        local,
        mesh=mesh,
        in_specs=(P("seq", None), P("seq", None), P("seq", None), P("seq")),
        out_specs=P("seq", None),
        check_vma=False,
    )
```

profile of v0, /device:TPU:504, one launch (start us, length us, event | category | flops | bytes accessed | tf_op | source)
XLA Modules:
  0.0 189.7 jit_solution(4373710588118249982)
XLA Ops:
  0.0 2.4 %copy.41 = bf16[512,1024]{0,1:T(8,128)(2,1)} copy(bf16[512,1024]{1,0:T(8,128)(2,1)} %param.14) | data formatting | bytes 2097152
  2.4 1.9 %collective-permute-start.3 = (bf16[512,1024]{0,1:T(8,128)(2,1)}, bf16[512,1024]{0,1:T(8,128)(2,1)}, u32[]{:S(2)}, u32[]{:S(2)}) collective-permute-start(bf16[512,1024]{0,1:T(8,128)(2,1)} %copy.41), channel_id=1, source_target_pairs={{511,0},{0,1},{1,2},{2,3},{3,4},{4,5},{5,6},{6,7},{7,8},{8,9},{9,1... | collective-permute-start | bytes 3145736 | tf_op jit(solution)/shard_map/ppermute | solution.py:15
  4.3 3.4 %collective-permute-start.8 = (bf16[512,1024]{0,1:T(8,128)(2,1)}, bf16[512,1024]{0,1:T(8,128)(2,1)}, u32[]{:S(2)}, u32[]{:S(2)}) collective-permute-start(bf16[512,1024]{0,1:T(8,128)(2,1)} %copy.41), channel_id=1, source_target_pairs={{384,0},{385,1},{386,2},{387,3},{388,4},{389,5},{390,6},{391,7},{3... | collective-permute-start | bytes 3145736 | tf_op jit(solution)/shard_map/ppermute | solution.py:15
  7.7 2.3 %copy.40 = bf16[512,1024]{0,1:T(8,128)(2,1)} copy(bf16[512,1024]{1,0:T(8,128)(2,1)} %param.16) | data formatting | bytes 2097152
  10.0 1.9 %collective-permute-start = (bf16[512,1024]{0,1:T(8,128)(2,1)}, bf16[512,1024]{0,1:T(8,128)(2,1)}, u32[]{:S(2)}, u32[]{:S(2)}) collective-permute-start(bf16[512,1024]{0,1:T(8,128)(2,1)} %copy.40), channel_id=1, source_target_pairs={{511,0},{0,1},{1,2},{2,3},{3,4},{4,5},{5,6},{6,7},{7,8},{8,9},{9,1... | collective-permute-start | bytes 3145736 | tf_op jit(solution)/shard_map/ppermute | solution.py:15
  11.9 1.3 copy.42
  13.2 1.9 %collective-permute-start.2 = (bf16[512,1024]{0,1:T(8,128)(2,1)}, bf16[512,1024]{0,1:T(8,128)(2,1)}, u32[]{:S(2)}, u32[]{:S(2)}) collective-permute-start(bf16[512,1024]{0,1:T(8,128)(2,1)} %copy.42), channel_id=1, source_target_pairs={{511,0},{0,1},{1,2},{2,3},{3,4},{4,5},{5,6},{6,7},{7,8},{8,9},{9,1... | collective-permute-start | bytes 3145736 | tf_op jit(solution)/shard_map/ppermute | solution.py:15
  15.1 1.9 %collective-permute-start.1 = (s32[1]{0:T(128)}, s32[1]{0:T(128)}, u32[]{:S(2)}, u32[]{:S(2)}) collective-permute-start(s32[1]{0:T(128)} %param.17), channel_id=1, source_target_pairs={{511,0},{0,1},{1,2},{2,3},{3,4},{4,5},{5,6},{6,7},{7,8},{8,9},{9,1... | collective-permute-start | bytes 20 | tf_op jit(solution)/shard_map/ppermute | solution.py:15
  17.2 21.4 %while.80 = (s32[]{:T(128)}, bf16[512,1024]{0,1:T(8,128)(2,1)S(1)}, f32[16,512]{1,0:T(8,128)S(1)}, bf16[512,1024]{0,1:T(8,128)(2,1)}, bf16[512,1024]{0,1:T(8,128...) while((s32[]{:T(128)}, bf16[512,1024]{0,1:T(8,128)(2,1)S(1)}, ...), condition=%wide.region_3.4_spmd.clone, body=%wide.region_0.3_spmd.clone.sunk | while | flops 278133248 | bytes 15787757 | solution.py:63
  38.6 3.4 %collective-permute-start.5 = (bf16[512,1024]{0,1:T(8,128)(2,1)}, bf16[512,1024]{0,1:T(8,128)(2,1)}, u32[]{:S(2)}, u32[]{:S(2)}) collective-permute-start(bf16[512,1024]{0,1:T(8,128)(2,1)} %copy.40), channel_id=1, source_target_pairs={{384,0},{385,1},{386,2},{387,3},{388,4},{389,5},{390,6},{391,7},{3... | collective-permute-start | bytes 3145736 | tf_op jit(solution)/shard_map/ppermute | solution.py:15
  42.1 21.4 %while.82 = (s32[]{:T(128)}, bf16[512,1024]{0,1:T(8,128)(2,1)S(1)}, f32[16,512]{1,0:T(8,128)S(1)}, bf16[512,1024]{0,1:T(8,128)(2,1)}, bf16[512,1024]{0,1:T(8,128...) while((s32[]{:T(128)}, bf16[512,1024]{0,1:T(8,128)(2,1)S(1)}, ...), condition=%wide.region_11.12_spmd.clone, body=%wide.region_8.11_spmd.clone.sunk | while | flops 278133248 | bytes 15787757 | solution.py:63
  63.5 3.1 %collective-permute-start.7 = (bf16[512,1024]{0,1:T(8,128)(2,1)}, bf16[512,1024]{0,1:T(8,128)(2,1)}, u32[]{:S(2)}, u32[]{:S(2)}) collective-permute-start(bf16[512,1024]{0,1:T(8,128)(2,1)} %copy.42), channel_id=1, source_target_pairs={{384,0},{385,1},{386,2},{387,3},{388,4},{389,5},{390,6},{391,7},{3... | collective-permute-start | bytes 3145736 | tf_op jit(solution)/shard_map/ppermute | solution.py:15
  67.7 24.1 %while.84 = (s32[]{:T(128)}, bf16[512,1024]{0,1:T(8,128)(2,1)}, f32[16,512]{1,0:T(8,128)S(1)}, bf16[512,1024]{0,1:T(8,128)(2,1)}, bf16[512,1024]{0,1:T(8,128)(2,...) while((s32[]{:T(128)}, bf16[512,1024]{0,1:T(8,128)(2,1)}, ...), condition=%wide.region_19.20_spmd.clone, body=%wide.region_16.19_spmd.clone.sunk | while | flops 278133248 | bytes 15787757 | solution.py:63
  91.7 2.4 %collective-permute-start.6 = (s32[1]{0:T(128)}, s32[1]{0:T(128)}, u32[]{:S(2)}, u32[]{:S(2)}) collective-permute-start(s32[1]{0:T(128)} %param.17), channel_id=1, source_target_pairs={{384,0},{385,1},{386,2},{387,3},{388,4},{389,5},{390,6},{391,7},{3... | collective-permute-start | bytes 20 | tf_op jit(solution)/shard_map/ppermute | solution.py:15
  94.1 2.8 %collective-permute-start.4 = (f32[16,512]{1,0:T(8,128)S(1)}, f32[16,512]{1,0:T(8,128)S(1)}, u32[]{:S(2)}, u32[]{:S(2)}) collective-permute-start(f32[16,512]{1,0:T(8,128)S(1)} %get-tuple-element.633), channel_id=1, source_target_pairs={{1,0},{2,1},{3,2},{4,3},{5,4},{6,5},{7,6},{8,7},{9,8},{10,9},{11,1... | collective-permute-start | bytes 98312 | tf_op jit(solution)/shard_map/ppermute | solution.py:15
  96.9 4.8 %collective-permute-start.9 = (f32[16,512]{1,0:T(8,128)S(1)}, f32[16,512]{1,0:T(8,128)S(1)}, u32[]{:S(2)}, u32[]{:S(2)}) collective-permute-start(f32[16,512]{1,0:T(8,128)S(1)} %get-tuple-element.635), channel_id=1, source_target_pairs={{128,0},{129,1},{130,2},{131,3},{132,4},{133,5},{134,6},{135,7},{1... | collective-permute-start | bytes 98312 | tf_op jit(solution)/shard_map/ppermute | solution.py:15
  101.9 21.0 %while.81 = (s32[]{:T(128)}, bf16[512,1024]{0,1:T(8,128)(2,1)S(1)}, f32[16,512]{1,0:T(8,128)S(1)}, bf16[512,1024]{0,1:T(8,128)(2,1)}, bf16[512,1024]{0,1:T(8,128...) while((s32[]{:T(128)}, bf16[512,1024]{0,1:T(8,128)(2,1)S(1)}, ...), condition=%wide.region_7.8_spmd.clone, body=%wide.region_4.7_spmd.clone.sunk | while | flops 278133248 | bytes 15787757 | solution.py:63
  123.9 21.0 %while.83 = (s32[]{:T(128)}, bf16[512,1024]{0,1:T(8,128)(2,1)S(1)}, f32[16,512]{1,0:T(8,128)S(1)}, bf16[512,1024]{0,1:T(8,128)(2,1)}, bf16[512,1024]{0,1:T(8,128...) while((s32[]{:T(128)}, bf16[512,1024]{0,1:T(8,128)(2,1)S(1)}, ...), condition=%wide.region_15.16_spmd.clone, body=%wide.region_12.15_spmd.clone.sunk | while | flops 278133248 | bytes 15787757 | solution.py:63
  144.9 3.0 %collective-permute-start.10 = (bf16[512,1024]{0,1:T(8,128)(2,1)}, bf16[512,1024]{0,1:T(8,128)(2,1)S(1)}, u32[]{:S(2)}, u32[]{:S(2)}) collective-permute-start(bf16[512,1024]{0,1:T(8,128)(2,1)} %copy-done.3), channel_id=1, source_target_pairs={{1,0},{2,1},{3,2},{4,3},{5,4},{6,5},{7,6},{8,7},{9,8},{10,9},{11,1... | collective-permute-start | bytes 3145736 | tf_op jit(solution)/shard_map/ppermute | solution.py:15
  147.9 2.7 %collective-permute-start.11 = (bf16[512,1024]{0,1:T(8,128)(2,1)}, bf16[512,1024]{0,1:T(8,128)(2,1)S(1)}, u32[]{:S(2)}, u32[]{:S(2)}) collective-permute-start(bf16[512,1024]{0,1:T(8,128)(2,1)} %get-tuple-element.639), channel_id=1, source_target_pairs={{128,0},{129,1},{130,2},{131,3},{132,4},{133,5},{134,6},{135,7},{1... | collective-permute-start | bytes 3145736 | tf_op jit(solution)/shard_map/ppermute | solution.py:15
  150.8 9.7 %collective-permute-done.10 = bf16[512,1024]{0,1:T(8,128)(2,1)S(1)} collective-permute-done((bf16[512,1024]{0,1:T(8,128)(2,1)}, bf16[512,1024]{0,1:T(8,128)(2,1)S(1)}, u32[]{:S(2)}, u32[]{:S(2)}) %collective-permute-start.10) | collective-permute-done | bytes 1048608 | tf_op jit(solution)/shard_map/ppermute | solution.py:15
  160.5 25.2 %collective-permute-done.11 = bf16[512,1024]{0,1:T(8,128)(2,1)S(1)} collective-permute-done((bf16[512,1024]{0,1:T(8,128)(2,1)}, bf16[512,1024]{0,1:T(8,128)(2,1)S(1)}, u32[]{:S(2)}, u32[]{:S(2)}) %collective-permute-start.11) | collective-permute-done | bytes 1048608 | tf_op jit(solution)/shard_map/ppermute | solution.py:15
  185.8 2.6 %fusion.25 = bf16[512,1024]{0,1:T(8,128)(2,1)S(1)} fusion(bf16[512,1024]{0,1:T(8,128)(2,1)S(1)} %collective-permute-done.11, bf16[512,1024]{0,1:T(8,128)(2,1)S(1)} %get-tuple-element.638, bf16[512,1024]{0,1:T(8,128)(2,1)S(1)} %collective-permute-done.10, bf16[512,1024]{0,1:T(8,128)(2,1)} %copy-done.1, bf16[512,1024]{0,1:T(8,128)(2,1)} %copy-done, ...), kind=kLoop, calls=%fused_computation.71 | loop fusion | flops 8388608 | bytes 6488064 | tf_op jit(solution)/shard_map/convert_element_type | solution.py:77
  188.4 1.3 copy.55
  (196 shorter events, 109.9 us)
Async XLA Ops:
  0.0 11.9 %copy-start.2 = (bf16[512,1024]{1,0:T(8,128)(2,1)S(1)}, bf16[512,1024]{1,0:T(8,128)(2,1)}, u32[]{:S(2)}) copy-start(bf16[512,1024]{1,0:T(8,128)(2,1)} %param.15) | copy-start | bytes 3145732
  2.4 36.2 %collective-permute-start.3 = (bf16[512,1024]{0,1:T(8,128)(2,1)}, bf16[512,1024]{0,1:T(8,128)(2,1)}, u32[]{:S(2)}, u32[]{:S(2)}) collective-permute-start(bf16[512,1024]{0,1:T(8,128)(2,1)} %copy.41), channel_id=1, source_target_pairs={{511,0},{0,1},{1,2},{2,3},{3,4},{4,5},{5,6},{6,7},{7,8},{8,9},{9,1... | collective-permute-start | bytes 3145736 | tf_op jit(solution)/shard_map/ppermute | solution.py:15
  4.3 59.2 %collective-permute-start.8 = (bf16[512,1024]{0,1:T(8,128)(2,1)}, bf16[512,1024]{0,1:T(8,128)(2,1)}, u32[]{:S(2)}, u32[]{:S(2)}) collective-permute-start(bf16[512,1024]{0,1:T(8,128)(2,1)} %copy.41), channel_id=1, source_target_pairs={{384,0},{385,1},{386,2},{387,3},{388,4},{389,5},{390,6},{391,7},{3... | collective-permute-start | bytes 3145736 | tf_op jit(solution)/shard_map/ppermute | solution.py:15
  10.0 84.1 %collective-permute-start = (bf16[512,1024]{0,1:T(8,128)(2,1)}, bf16[512,1024]{0,1:T(8,128)(2,1)}, u32[]{:S(2)}, u32[]{:S(2)}) collective-permute-start(bf16[512,1024]{0,1:T(8,128)(2,1)} %copy.40), channel_id=1, source_target_pairs={{511,0},{0,1},{1,2},{2,3},{3,4},{4,5},{5,6},{6,7},{7,8},{8,9},{9,1... | collective-permute-start | bytes 3145736 | tf_op jit(solution)/shard_map/ppermute | solution.py:15
  13.2 83.7 %collective-permute-start.2 = (bf16[512,1024]{0,1:T(8,128)(2,1)}, bf16[512,1024]{0,1:T(8,128)(2,1)}, u32[]{:S(2)}, u32[]{:S(2)}) collective-permute-start(bf16[512,1024]{0,1:T(8,128)(2,1)} %copy.42), channel_id=1, source_target_pairs={{511,0},{0,1},{1,2},{2,3},{3,4},{4,5},{5,6},{6,7},{7,8},{8,9},{9,1... | collective-permute-start | bytes 3145736 | tf_op jit(solution)/shard_map/ppermute | solution.py:15
  15.1 76.6 %collective-permute-start.1 = (s32[1]{0:T(128)}, s32[1]{0:T(128)}, u32[]{:S(2)}, u32[]{:S(2)}) collective-permute-start(s32[1]{0:T(128)} %param.17), channel_id=1, source_target_pairs={{511,0},{0,1},{1,2},{2,3},{3,4},{4,5},{5,6},{6,7},{7,8},{8,9},{9,1... | collective-permute-start | bytes 20 | tf_op jit(solution)/shard_map/ppermute | solution.py:15
  38.6 3.5 %copy-start = (bf16[512,1024]{0,1:T(8,128)(2,1)}, bf16[512,1024]{0,1:T(8,128)(2,1)S(1)}, u32[]{:S(2)}) copy-start(bf16[512,1024]{0,1:T(8,128)(2,1)S(1)} %get-tuple-element.630) | copy-start | bytes 3145732
  38.6 84.3 %collective-permute-start.5 = (bf16[512,1024]{0,1:T(8,128)(2,1)}, bf16[512,1024]{0,1:T(8,128)(2,1)}, u32[]{:S(2)}, u32[]{:S(2)}) collective-permute-start(bf16[512,1024]{0,1:T(8,128)(2,1)} %copy.40), channel_id=1, source_target_pairs={{384,0},{385,1},{386,2},{387,3},{388,4},{389,5},{390,6},{391,7},{3... | collective-permute-start | bytes 3145736 | tf_op jit(solution)/shard_map/ppermute | solution.py:15
  63.5 4.2 %copy-start.3 = (bf16[512,1024]{0,1:T(8,128)(2,1)}, bf16[512,1024]{0,1:T(8,128)(2,1)S(1)}, u32[]{:S(2)}) copy-start(bf16[512,1024]{0,1:T(8,128)(2,1)S(1)} %get-tuple-element.637) | copy-start | bytes 3145732
  63.5 59.4 %collective-permute-start.7 = (bf16[512,1024]{0,1:T(8,128)(2,1)}, bf16[512,1024]{0,1:T(8,128)(2,1)}, u32[]{:S(2)}, u32[]{:S(2)}) collective-permute-start(bf16[512,1024]{0,1:T(8,128)(2,1)} %copy.42), channel_id=1, source_target_pairs={{384,0},{385,1},{386,2},{387,3},{388,4},{389,5},{390,6},{391,7},{3... | collective-permute-start | bytes 3145736 | tf_op jit(solution)/shard_map/ppermute | solution.py:15
  91.7 31.2 %collective-permute-start.6 = (s32[1]{0:T(128)}, s32[1]{0:T(128)}, u32[]{:S(2)}, u32[]{:S(2)}) collective-permute-start(s32[1]{0:T(128)} %param.17), channel_id=1, source_target_pairs={{384,0},{385,1},{386,2},{387,3},{388,4},{389,5},{390,6},{391,7},{3... | collective-permute-start | bytes 20 | tf_op jit(solution)/shard_map/ppermute | solution.py:15
  94.1 56.5 %collective-permute-start.4 = (f32[16,512]{1,0:T(8,128)S(1)}, f32[16,512]{1,0:T(8,128)S(1)}, u32[]{:S(2)}, u32[]{:S(2)}) collective-permute-start(f32[16,512]{1,0:T(8,128)S(1)} %get-tuple-element.633), channel_id=1, source_target_pairs={{1,0},{2,1},{3,2},{4,3},{5,4},{6,5},{7,6},{8,7},{9,8},{10,9},{11,1... | collective-permute-start | bytes 98312 | tf_op jit(solution)/shard_map/ppermute | solution.py:15
  96.9 53.8 %collective-permute-start.9 = (f32[16,512]{1,0:T(8,128)S(1)}, f32[16,512]{1,0:T(8,128)S(1)}, u32[]{:S(2)}, u32[]{:S(2)}) collective-permute-start(f32[16,512]{1,0:T(8,128)S(1)} %get-tuple-element.635), channel_id=1, source_target_pairs={{128,0},{129,1},{130,2},{131,3},{132,4},{133,5},{134,6},{135,7},{1... | collective-permute-start | bytes 98312 | tf_op jit(solution)/shard_map/ppermute | solution.py:15
  122.9 1.0 copy-start.1
  144.9 15.6 %collective-permute-start.10 = (bf16[512,1024]{0,1:T(8,128)(2,1)}, bf16[512,1024]{0,1:T(8,128)(2,1)S(1)}, u32[]{:S(2)}, u32[]{:S(2)}) collective-permute-start(bf16[512,1024]{0,1:T(8,128)(2,1)} %copy-done.3), channel_id=1, source_target_pairs={{1,0},{2,1},{3,2},{4,3},{5,4},{6,5},{7,6},{8,7},{9,8},{10,9},{11,1... | collective-permute-start | bytes 3145736 | tf_op jit(solution)/shard_map/ppermute | solution.py:15
  147.9 37.9 %collective-permute-start.11 = (bf16[512,1024]{0,1:T(8,128)(2,1)}, bf16[512,1024]{0,1:T(8,128)(2,1)S(1)}, u32[]{:S(2)}, u32[]{:S(2)}) collective-permute-start(bf16[512,1024]{0,1:T(8,128)(2,1)} %get-tuple-element.639), channel_id=1, source_target_pairs={{128,0},{129,1},{130,2},{131,3},{132,4},{133,5},{134,6},{135,7},{1... | collective-permute-start | bytes 3145736 | tf_op jit(solution)/shard_map/ppermute | solution.py:15
where the time goes:
time: 191 us; the launch traced here: 190 us
  local copies, waits for them, and re-layouts  53.7 us (28%)
  other arithmetic  36.4 us (19%)
  waiting for transfers between devices  35 us (18%)
  starting transfers between devices  33.3 us (17%)
  matrix products  29.6 us (15%)
    ppermute x12, waiting for transfers between devices, passed_along(): return lax.ppermute(block, axis, route)  35 us
    ppermute x12, starting transfers between devices, passed_along(): return lax.ppermute(block, axis, route)  33.3 us
    dynamic_slice x20, local copies, waits for them, and re-layouts, head_pass(): lax.dynamic_slice_in_dim(key_block, first_column, slab_width, 1)  21.4 us
    reduce_sum x20, other arithmetic, head_pass(): totals = jnp.sum(weights.astype(jnp.float32), axis=-1)  21 us
    dot_general x20, matrix products, head_pass(): jnp.einsum('thd,shd->hts', query_slab, key_slab, preferred_element_type=j...  20.5 us
    dynamic_slice x20, local copies, waits for them, and re-layouts, head_pass(): lax.dynamic_slice_in_dim(value_block, first_column, slab_width, 1)  19.5 us
    lt x20, other arithmetic, attend_block(): visible = jnp.arange(key_count) < length  12.3 us
    dot_general x20, matrix products, head_pass(): jnp.einsum('hts,shd->thd', weights, value_slab, preferred_element_type=jn...  9.1 us
  transfers between devices with their start and end apart: 12, of which 2 were waited for; matrix products, arithmetic and copies ran while one was open for 59% of the time, Pallas kernels for 0%

commit v1 on v0

v1 whole, which is shorter than its diff:
```python
import functools
import math

import jax
import jax.numpy as jnp
from jax import lax
from jax.experimental import pallas as pl
from jax.experimental.pallas import tpu as pltpu
from jax.sharding import PartitionSpec as P

MESH = pl.DeviceIdType.MESH
HEAD_DIM = 64
LANES = 128
PLANE = 128
RELAYS = 16
HOP_STEP = (5, 4)
UP, DOWN, SAME, OFF = range(4)
GAIN = math.log2(math.e) / math.sqrt(HEAD_DIM)
BF16 = jnp.bfloat16
F32 = jnp.float32


RELAY_AT = (
    (2, 1, 1), (5, 1, 1), (7, 6, 1), (6, 0, 1), (1, 0, 1), (6, 6, 1), (7, 5, 1), (4, 1, 1),
    (0, 0, 1), (5, 0, 1), (0, 1, 1), (5, 6, 1), (2, 0, 1), (6, 1, 1), (3, 0, 1), (4, 0, 1),
)


def relay_place(flow, g):
    y, z, core = RELAY_AT[g]
    place = (y * 8 + z) * 2 + core
    return place if flow == 0 else PLANE - 1 - place


def kernel(
    count, len_ref, q_hbm, k_hbm, v_hbm, out_hbm,
    q_own, kv_own, kv_in, out_own, lens, bias, k_aug, v_aug, probs, acc, tot, peak, relay,
    own_sem, send_sem, recv_sem, len_send, len_recv, piece_sem, hop_recv, hop_send, out_sem, ready, off_ready,
):
    rows, width = q_own.shape
    strips = width // LANES
    me = lax.axis_index("seq")
    core = lax.rem(me, 2)
    place = lax.rem(me, PLANE)
    plane = me - place
    above = lax.rem(plane + PLANE, count)
    below = lax.rem(plane + count - PLANE, count)
    partners = [
        lax.rem(me + PLANE, count),
        lax.rem(me + count - PLANE, count),
        me + 1 - 2 * core,
        lax.rem(me + count - 1 + 2 * core, count),
    ]
    first, last = place == 0, place == PLANE - 1
    inner = jnp.logical_not(jnp.logical_or(first, last))
    is_relay, piece = [], []
    for flow in range(2):
        hits = [place == relay_place(flow, g) for g in range(RELAYS)]
        is_relay.append(functools.reduce(jnp.logical_or, hits))
        piece.append(sum(jnp.where(hit, g, 0) for g, hit in enumerate(hits)))

    def strip_of(j):
        if isinstance(j, int):
            return pl.ds(j * LANES, LANES)
        return pl.ds(pl.multiple_of(j * LANES, LANES), LANES)

    def remote(src, dst, send, recv, device):
        return pltpu.make_async_remote_copy(
            src_ref=src, dst_ref=dst, send_sem=send, recv_sem=recv, device_id=(device,), device_id_type=MESH
        )

    def strip_copy(slot, t, j):
        src = (k_hbm, v_hbm)[t]
        return remote(
            src.at[:, strip_of(j)], kv_in.at[slot, t, :, strip_of(j)],
            send_sem.at[slot, t, j], recv_sem.at[slot, t, j], partners[slot],
        )

    def len_copy(slot):
        return remote(lens.at[4], lens.at[slot], len_send.at[slot], len_recv.at[slot], partners[slot])

    def piece_copy(flow, g):
        src = (k_hbm, v_hbm)[g % 2]
        return remote(
            src.at[:, strip_of(g // 2)], relay.at[flow], piece_sem.at[g], hop_recv.at[flow],
            (above, below)[flow] + relay_place(flow, g),
        )

    def hop_copy(flow):
        t, j = lax.rem(piece[flow], 2), lax.div(piece[flow], 2)
        return remote(
            relay.at[flow], kv_in.at[OFF, t, :, strip_of(j)], hop_send.at[flow], recv_sem.at[OFF, t, j],
            plane + (0, PLANE - 1)[flow],
        )

    def signal(semaphore, device):
        pl.semaphore_signal(semaphore, inc=1, device_id=(device,), device_id_type=MESH)

    local = [
        pltpu.make_async_copy(q_hbm, q_own, own_sem.at[0]),
        pltpu.make_async_copy(k_hbm, kv_own.at[0], own_sem.at[1]),
        pltpu.make_async_copy(v_hbm, kv_own.at[1], own_sem.at[2]),
    ]
    barrier = pltpu.get_barrier_semaphore()
    for slot in (UP, DOWN, SAME):
        signal(barrier, partners[slot])

    @pl.when(core == 0)
    def _():
        signal(barrier, partners[OFF])

    @pl.when(first)
    def _():
        for g in range(RELAYS):
            signal(barrier, plane + relay_place(0, g))
            signal(barrier, below + relay_place(1, g))

    @pl.when(last)
    def _():
        for g in range(RELAYS):
            signal(barrier, plane + relay_place(1, g))

    @pl.when(is_relay[0])
    def _():
        signal(barrier, below + PLANE - 1)

    for copy in local:
        copy.start()
    lens[4] = jnp.full(lens.shape[1:], len_ref[0], jnp.int32)
    pl.semaphore_wait(
        barrier,
        3 + core + jnp.where(last, RELAYS, 0) + jnp.where(is_relay[0], 1, 0) + jnp.where(is_relay[1], 2, 0),
    )

    @pl.when(core == 1)
    def _():
        signal(off_ready, partners[OFF])

    @pl.when(is_relay[1])
    def _():
        signal(ready, above)

    def start_pieces(flow):
        for g in range(RELAYS):
            piece_copy(flow, g).start()

    def start_off():
        len_copy(OFF).start()

        @pl.when(inner)
        def _():
            for j in range(strips):
                for t in range(2):
                    strip_copy(OFF, t, j).start()

    pl.when(last)(functools.partial(start_pieces, 0))
    for slot in (UP, DOWN, SAME):
        len_copy(slot).start()
    for j in range(strips):
        for slot in (UP, DOWN, SAME):
            for t in range(2):
                strip_copy(slot, t, j).start()
    pl.when(core == 1)(start_off)

    for copy in local:
        copy.wait()
    position = lax.broadcasted_iota(jnp.int32, (rows, LANES), 0)

    def take_mask(block):
        bias[block] = jnp.where(position < lens[block, 0:1, :], 0.0, -1e30).astype(BF16)

    take_mask(4)
    len_copy(SAME).wait_recv()
    take_mask(SAME)

    lane = lax.broadcasted_iota(jnp.int32, (rows, LANES), 1)
    low = lane < HEAD_DIM
    ones = jnp.ones((rows, LANES), BF16)
    marks = ((lane == HEAD_DIM).astype(BF16), (lane == 0).astype(BF16))

    def block_view(block, t, j):
        return kv_own[t, :, strip_of(j)] if block == 4 else kv_in[block, t, :, strip_of(j)]

    def take_keys(blocks, j):
        for i, block in enumerate(blocks):
            keys, mask = block_view(block, 0, j), bias[block]
            at = pl.ds(i * rows, rows)
            k_aug[0, at] = jnp.where(low, keys, mask)
            k_aug[1, at] = jnp.where(low, mask, keys)

    def take_values(blocks, j):
        for i, block in enumerate(blocks):
            values = block_view(block, 1, j)
            at = pl.ds(i * rows, rows)
            v_aug[0, at] = jnp.where(low, values, ones)
            v_aug[1, at] = jnp.where(low, ones, values)

    def score(head, n, j):
        q = q_own[:, strip_of(j)]
        q = jnp.where(low, q, marks[0]) if head == 0 else jnp.where(low, marks[1], q)
        return lax.dot_general(
            q, k_aug[head, 0 : n * rows], (((1,), (1,)), ((), ())), preferred_element_type=F32
        )

    def weigh(scores):
        top = jnp.max(scores, axis=1, keepdims=True)
        return jnp.exp2((scores - top) * GAIN).astype(BF16), top

    def blend(head, n, weights):
        return jnp.dot(weights, v_aug[head, 0 : n * rows], preferred_element_type=F32)

    def joined(pair, tops):
        blended = jnp.where(low, pair[0], pair[1])
        totals = pltpu.roll(jnp.where(low, pair[1], pair[0]), HEAD_DIM, 1)
        return blended, totals, jnp.where(low, tops[0], tops[1])

    def attend(blocks, j):
        take_keys(blocks, j)
        take_values(blocks, j)
        n = len(blocks)
        scores = [score(head, n, j) for head in range(2)]
        weights, tops = zip(*[weigh(s) for s in scores])
        return joined([blend(head, n, weights[head]) for head in range(2)], tops)

    def merged(j, blended, totals, top):
        ceiling = jnp.maximum(peak[j], top)
        old, new = jnp.exp2((peak[j] - ceiling) * GAIN), jnp.exp2((top - ceiling) * GAIN)
        return acc[j] * old + blended * new, tot[j] * old + totals * new, ceiling

    def keep(j, state):
        acc[j], tot[j], peak[j] = state

    def out_copy(j):
        return pltpu.make_async_copy(
            out_own.at[:, strip_of(j)], out_hbm.at[:, strip_of(j)], out_sem.at[j]
        )

    def finish(j, state):
        out_own[:, strip_of(j)] = (state[0] / state[1]).astype(BF16)
        out_copy(j).start()

    def arrived(slots, j, parts=(0, 1)):
        for slot in slots:
            for t in parts:
                strip_copy(slot, t, j).wait_recv()

    def pass_on(step):
        for flow in range(2):

            @pl.when(jnp.logical_and(is_relay[flow], step == HOP_STEP[flow] + lax.div(3 * piece[flow], 8)))
            def _():
                piece_copy(flow, 0).wait_recv()
                hop_copy(flow).start()

    @pl.loop(0, strips)
    def _(j):
        arrived([SAME], j)
        keep(j, attend([4, SAME], j))

        @pl.when(jnp.logical_and(core == 0, j == 0))
        def _():
            pl.semaphore_wait(off_ready, 1)
            start_off()

        @pl.when(jnp.logical_and(first, j == 0))
        def _():
            pl.semaphore_wait(ready, RELAYS)
            start_pieces(1)

        pass_on(j)

    for slot in (UP, DOWN, OFF):
        len_copy(slot).wait_recv()
        take_mask(slot)

    @pl.loop(0, strips - 1)
    def _(j):
        arrived([OFF, UP, DOWN], j)
        finish(j, merged(j, *attend([OFF, UP, DOWN], j)))
        pass_on(strips + j)

    end = strips - 1
    arrived([OFF], end)
    keep(end, merged(end, *attend([OFF], end)))
    arrived([UP, DOWN], end, (0,))
    take_keys([UP, DOWN], end)
    tops = []
    for head, scores in enumerate([score(head, 2, end) for head in range(2)]):
        probs[head], top = weigh(scores)
        tops.append(top)
    arrived([UP, DOWN], end, (1,))
    take_values([UP, DOWN], end)
    pair = [blend(head, 2, probs[head]) for head in range(2)]
    finish(end, merged(end, *joined(pair, tops)))

    for slot in range(4):
        len_copy(slot).wait_send()
    for j in range(strips):
        for slot in (UP, DOWN, SAME):
            for t in range(2):
                strip_copy(slot, t, j).wait_send()

        @pl.when(inner)
        def _():
            for t in range(2):
                strip_copy(OFF, t, j).wait_send()

    for flow in range(2):

        @pl.when(is_relay[flow])
        def _():
            hop_copy(flow).wait_send()

    @pl.when(jnp.logical_not(inner))
    def _():
        for g in range(RELAYS):
            piece_copy(0, g).wait_send()

    for j in range(strips):
        out_copy(j).wait()


def local(count, queries, keys, values, lengths):
    rows, width = queries.shape
    strips = width // LANES
    hbm = pl.BlockSpec(memory_space=pl.ANY)
    dma = pltpu.SemaphoreType.DMA
    return pl.pallas_call(
        functools.partial(kernel, count),
        out_shape=jax.ShapeDtypeStruct((rows, width), BF16),
        in_specs=[pl.BlockSpec(memory_space=pltpu.SMEM), hbm, hbm, hbm],
        out_specs=hbm,
        scratch_shapes=[
            pltpu.VMEM((rows, width), BF16),
            pltpu.VMEM((2, rows, width), BF16),
            pltpu.VMEM((4, 2, rows, width), BF16),
            pltpu.VMEM((rows, width), BF16),
            pltpu.VMEM((5, 8, LANES), jnp.int32),
            pltpu.VMEM((5, rows, LANES), BF16),
            pltpu.VMEM((2, 3 * rows, LANES), BF16),
            pltpu.VMEM((2, 3 * rows, LANES), BF16),
            pltpu.VMEM((2, rows, 2 * rows), BF16),
            pltpu.VMEM((strips, rows, LANES), F32),
            pltpu.VMEM((strips, rows, LANES), F32),
            pltpu.VMEM((strips, rows, LANES), F32),
            pltpu.VMEM((2, rows, LANES), BF16),
            dma((3,)),
            dma((4, 2, strips)),
            dma((4, 2, strips)),
            dma((4,)),
            dma((4,)),
            dma((RELAYS,)),
            dma((2,)),
            dma((2,)),
            dma((strips,)),
            pltpu.SemaphoreType.REGULAR,
            pltpu.SemaphoreType.REGULAR,
        ],
        compiler_params=pltpu.CompilerParams(
            collective_id=0, has_side_effects=True, vmem_limit_bytes=56 << 20
        ),
        cost_estimate=pl.CostEstimate(
            flops=20 * rows * rows * width, bytes_accessed=12 * rows * width, transcendentals=80 * rows * rows
        ),
    )(lengths, queries, keys, values)


def solution(mesh):
    return jax.shard_map(
        functools.partial(local, mesh.shape["seq"]),
        mesh=mesh,
        in_specs=(P("seq", None), P("seq", None), P("seq", None), P("seq")),
        out_specs=P("seq", None),
        check_vma=False,
    )
```

time: 191 us -> 61.9 us (0.32)
  the two profiles are of different devices: /device:TPU:504 before, /device:TPU:66 now
where the time goes in v1:
time: 61.9 us; the launch traced here: 61.7 us
  Pallas kernels  58.8 us (95%)
  local copies, waits for them, and re-layouts  2.26 us (4%)
  between operations  0.66 us (1%)
    pallas_call x1, Pallas kernels, local(): pl.pallas_call(functools.partial(kernel, count), out_shape=jax.ShapeDtype...  58.8 us
    unnamed x1, local copies, waits for them, and re-layouts  2.26 us

profile of v1, /device:TPU:66, one launch (start us, length us, event | category | flops | bytes accessed | tf_op | source)
XLA Modules:
  0.0 61.7 jit_solution(50759245545571661)
XLA Ops:
  0.7 58.8 %shard_map.46 = bf16[512,1024]{1,0:T(8,128)(2,1)} custom-call(s32[1]{0:T(128)S(6)} %copy.6.len_ref, bf16[512,1024]{1,0:T(8,128)(2,1)} %q_hbm.1, bf16[512,1024]{1,0:T(8,128)(2,1)} %k_hbm.1, bf16[512,1024]{1,0:T(8,128)(2,1)} %v_hbm.1), custom_call_target="tpu_custom_call" | custom-call | flops 5368709120 | bytes 6291456 | tf_op jit(solution)/shard_map/pallas_call | solution.py:328
  59.5 2.3 %copy.7 = bf16[512,1024]{1,0:T(8,128)(2,1)} copy(bf16[512,1024]{1,0:T(8,128)(2,1)} %shard_map.46) | data formatting | bytes 2097152

commit v2 on v1

--- a/solution.py
+++ b/solution.py
@@ -33,9 +33,9 @@
 
 
 def kernel(
-    count, len_ref, q_hbm, k_hbm, v_hbm, out_hbm,
-    q_own, kv_own, kv_in, out_own, lens, bias, k_aug, v_aug, probs, acc, tot, peak, relay,
-    own_sem, send_sem, recv_sem, len_send, len_recv, piece_sem, hop_recv, hop_send, out_sem, ready, off_ready,
+    count, len_ref, q_hbm, k_hbm, v_hbm, out_ref,
+    q_own, kv_own, kv_in, lens, bias, k_aug, v_aug, probs, acc, tot, peak, relay,
+    own_sem, send_sem, recv_sem, len_send, len_recv, piece_sem, hop_recv, hop_send, ready, off_ready, hop_ready,
 ):
     rows, width = q_own.shape
     strips = width // LANES
@@ -115,21 +115,20 @@
             signal(barrier, plane + relay_place(0, g))
             signal(barrier, below + relay_place(1, g))
 
-    @pl.when(last)
-    def _():
-        for g in range(RELAYS):
-            signal(barrier, plane + relay_place(1, g))
-
     @pl.when(is_relay[0])
     def _():
         signal(barrier, below + PLANE - 1)
+
+    @pl.when(is_relay[1])
+    def _():
+        signal(barrier, plane + PLANE - 1)
 
     for copy in local:
         copy.start()
     lens[4] = jnp.full(lens.shape[1:], len_ref[0], jnp.int32)
     pl.semaphore_wait(
         barrier,
-        3 + core + jnp.where(last, RELAYS, 0) + jnp.where(is_relay[0], 1, 0) + jnp.where(is_relay[1], 2, 0),
+        3 + core + jnp.where(last, 2 * RELAYS, 0) + sum(jnp.where(hit, 1, 0) for hit in is_relay),
     )
 
     @pl.when(core == 1)
@@ -139,6 +138,11 @@
     @pl.when(is_relay[1])
     def _():
         signal(ready, above)
+
+    @pl.when(last)
+    def _():
+        for g in range(RELAYS):
+            signal(hop_ready, plane + relay_place(1, g))
 
     def start_pieces(flow):
         for g in range(RELAYS):
@@ -230,14 +234,8 @@
     def keep(j, state):
         acc[j], tot[j], peak[j] = state
 
-    def out_copy(j):
-        return pltpu.make_async_copy(
-            out_own.at[:, strip_of(j)], out_hbm.at[:, strip_of(j)], out_sem.at[j]
-        )
-
     def finish(j, state):
-        out_own[:, strip_of(j)] = (state[0] / state[1]).astype(BF16)
-        out_copy(j).start()
+        out_ref[:, strip_of(j)] = (state[0] / state[1]).astype(BF16)
 
     def arrived(slots, j, parts=(0, 1)):
         for slot in slots:
@@ -250,6 +248,8 @@
             @pl.when(jnp.logical_and(is_relay[flow], step == HOP_STEP[flow] + lax.div(3 * piece[flow], 8)))
             def _():
                 piece_copy(flow, 0).wait_recv()
+                if flow == 1:
+                    pl.semaphore_wait(hop_ready, 1)
                 hop_copy(flow).start()
 
     @pl.loop(0, strips)
@@ -316,25 +316,21 @@
         for g in range(RELAYS):
             piece_copy(0, g).wait_send()
 
-    for j in range(strips):
-        out_copy(j).wait()
-
 
 def local(count, queries, keys, values, lengths):
     rows, width = queries.shape
     strips = width // LANES
-    hbm = pl.BlockSpec(memory_space=pl.ANY)
+    hbm = pl.BlockSpec(memory_space=pltpu.HBM)
     dma = pltpu.SemaphoreType.DMA
     return pl.pallas_call(
         functools.partial(kernel, count),
         out_shape=jax.ShapeDtypeStruct((rows, width), BF16),
         in_specs=[pl.BlockSpec(memory_space=pltpu.SMEM), hbm, hbm, hbm],
-        out_specs=hbm,
+        out_specs=pl.BlockSpec(memory_space=pltpu.VMEM),
         scratch_shapes=[
             pltpu.VMEM((rows, width), BF16),
             pltpu.VMEM((2, rows, width), BF16),
             pltpu.VMEM((4, 2, rows, width), BF16),
-            pltpu.VMEM((rows, width), BF16),
             pltpu.VMEM((5, 8, LANES), jnp.int32),
             pltpu.VMEM((5, rows, LANES), BF16),
             pltpu.VMEM((2, 3 * rows, LANES), BF16),
@@ -352,12 +348,12 @@
             dma((RELAYS,)),
             dma((2,)),
             dma((2,)),
-            dma((strips,)),
+            pltpu.SemaphoreType.REGULAR,
             pltpu.SemaphoreType.REGULAR,
             pltpu.SemaphoreType.REGULAR,
         ],
         compiler_params=pltpu.CompilerParams(
-            collective_id=0, has_side_effects=True, vmem_limit_bytes=56 << 20
+            collective_id=0, has_side_effects=True, vmem_limit_bytes=52 << 20
         ),
         cost_estimate=pl.CostEstimate(
             flops=20 * rows * rows * width, bytes_accessed=12 * rows * width, transcendentals=80 * rows * rows

time: 61.9 us -> 59.4 us (0.960)
  the two profiles are of different devices: /device:TPU:66 before, /device:TPU:64 now
where the time goes in v2:
time: 59.4 us; the launch traced here: 59.3 us
  Pallas kernels  57.6 us (97%)
  local copies, waits for them, and re-layouts  0.97 us (2%)
  between operations  0.66 us (1%)
    pallas_call x1, Pallas kernels, local(): pl.pallas_call(functools.partial(kernel, count), out_shape=jax.ShapeDtype...  57.6 us

profile of v2, /device:TPU:64, one launch (start us, length us, event | category | flops | bytes accessed | tf_op | source)
XLA Modules:
  0.0 59.3 jit_solution(2397149427397258608)
XLA Ops:
  0.7 57.6 %shard_map.46 = bf16[512,1024]{1,0:T(8,128)(2,1)S(1)} custom-call(s32[1]{0:T(128)S(6)} %copy.6.len_ref, bf16[512,1024]{1,0:T(8,128)(2,1)} %q_hbm.1, bf16[512,1024]{1,0:T(8,128)(2,1)} %k_hbm.1, bf16[512,1024]{1,0:T(8,128)(2,1)} %v_hbm.1), custom_call_target="tpu_custom_call" | custom-call | flops 5368709120 | bytes 6291456 | tf_op jit(solution)/shard_map/pallas_call | solution.py:325
  58.3 1.0 %copy.7 = bf16[512,1024]{1,0:T(8,128)(2,1)} copy(bf16[512,1024]{1,0:T(8,128)(2,1)S(1)} %shard_map.46) | data formatting | bytes 2097152

commit v3 on v2

--- a/solution.py
+++ b/solution.py
@@ -76,6 +76,14 @@
             send_sem.at[slot, t, j], recv_sem.at[slot, t, j], partners[slot],
         )
 
+    def wide_copy(slot, t, j):
+        src = (k_hbm, v_hbm)[t]
+        lanes = pl.ds(j * LANES if isinstance(j, int) else pl.multiple_of(j * LANES, LANES), 2 * LANES)
+        return remote(
+            src.at[:, lanes], kv_in.at[slot, t, :, lanes],
+            send_sem.at[slot, t, j], recv_sem.at[slot, t, j], partners[slot],
+        )
+
     def len_copy(slot):
         return remote(lens.at[4], lens.at[slot], len_send.at[slot], len_recv.at[slot], partners[slot])
 
@@ -161,9 +169,14 @@
     for slot in (UP, DOWN, SAME):
         len_copy(slot).start()
     for j in range(strips):
-        for slot in (UP, DOWN, SAME):
+        for t in range(2):
+            strip_copy(SAME, t, j).start()
+        for slot in (UP, DOWN):
             for t in range(2):
-                strip_copy(slot, t, j).start()
+                if j >= strips - 2:
+                    strip_copy(slot, t, j).start()
+                elif j % 2 == 0:
+                    wide_copy(slot, t, j).start()
     pl.when(core == 1)(start_off)
 
     for copy in local:
@@ -275,7 +288,18 @@
 
     @pl.loop(0, strips - 1)
     def _(j):
-        arrived([OFF, UP, DOWN], j)
+        arrived([OFF], j)
+
+        @pl.when(jnp.logical_and(lax.rem(j, 2) == 0, j < strips - 2))
+        def _():
+            for slot in (UP, DOWN):
+                for t in range(2):
+                    wide_copy(slot, t, j).wait_recv()
+
+        @pl.when(j == strips - 2)
+        def _():
+            arrived([UP, DOWN], strips - 2)
+
         finish(j, merged(j, *attend([OFF, UP, DOWN], j)))
         pass_on(strips + j)
 
@@ -296,9 +320,14 @@
     for slot in range(4):
         len_copy(slot).wait_send()
     for j in range(strips):
-        for slot in (UP, DOWN, SAME):
+        for t in range(2):
+            strip_copy(SAME, t, j).wait_send()
+        for slot in (UP, DOWN):
             for t in range(2):
-                strip_copy(slot, t, j).wait_send()
+                if j >= strips - 2:
+                    strip_copy(slot, t, j).wait_send()
+                elif j % 2 == 0:
+                    wide_copy(slot, t, j).wait_send()
 
         @pl.when(inner)
         def _():

time: 59.4 us -> 59.4 us (level)
  no operation moved by 1% of the time
where the time goes in v3:
time: 59.4 us; the launch traced here: 59.2 us
  Pallas kernels  57.6 us (97%)
  local copies, waits for them, and re-layouts  0.97 us (2%)
  between operations  0.66 us (1%)
    pallas_call x1, Pallas kernels, local(): pl.pallas_call(functools.partial(kernel, count), out_shape=jax.ShapeDtype...  57.6 us

profile of v3, /device:TPU:64, one launch (start us, length us, event | category | flops | bytes accessed | tf_op | source)
XLA Modules:
  0.0 59.2 jit_solution(11790964408210928023)
XLA Ops:
  0.7 57.6 %shard_map.46 = bf16[512,1024]{1,0:T(8,128)(2,1)S(1)} custom-call(s32[1]{0:T(128)S(6)} %copy.6.len_ref, bf16[512,1024]{1,0:T(8,128)(2,1)} %q_hbm.1, bf16[512,1024]{1,0:T(8,128)(2,1)} %k_hbm.1, bf16[512,1024]{1,0:T(8,128)(2,1)} %v_hbm.1), custom_call_target="tpu_custom_call" | custom-call | flops 5368709120 | bytes 6291456 | tf_op jit(solution)/shard_map/pallas_call | solution.py:354
  58.3 1.0 %copy.7 = bf16[512,1024]{1,0:T(8,128)(2,1)} copy(bf16[512,1024]{1,0:T(8,128)(2,1)S(1)} %shard_map.46) | data formatting | bytes 2097152
